TPU v7x, 32 devices: a whole 2x2x4 slice. The times are simulated.
32 devices in a mesh: group: 2 (over x), expert: 4 (over y, core), dp: 4 (over z).
Axes of the slice: x: 2, y: 2, z: 4, core: 2. Of those that a mesh axis runs over, the one named last changes fastest.
Arguments:
- tokens: bfloat16 [4608, 7168], P(('group', 'expert', 'dp')), parts along dimension 0, may hold values from -4 to 4
- counts: int32 [32], P(('group', 'expert', 'dp')), parts along dimension 0, may hold values from 0 to 144, as said below
- send_counts: int32 [32, 4], P(('group', 'expert', 'dp')), parts along dimension 0, may hold values from 0 to 48, as said below
- routes: int32 [4608, 8], P(('group', 'expert', 'dp')), parts along dimension 0, may hold values from 0 to 255, as said below
- route_weights: bfloat16 [4608, 8], P(('group', 'expert', 'dp')), parts along dimension 0, may hold values from 0.099609375 to 0.59765625
- norm_gain: bfloat16 [7168], replicated, may hold values from 0.099609375 to 1.8984375
- w_gate: bfloat16 [4, 7168, 1024], P('expert', None, 'dp'), may hold values from -0.0625 to 0.0625
- w_up: bfloat16 [4, 7168, 1024], P('expert', None, 'dp'), may hold values from -0.0625 to 0.0625
- w_down: bfloat16 [4, 1024, 7168], P('expert', 'dp'), may hold values from -0.1875 to 0.1875
Outputs:
- mixed: bfloat16 [3072, 7168], P(('group', 'expert', 'dp')), parts along dimension 0
There are 2 independent parts, one for each index of `group`. A program takes and returns all parts, laid end to end along the dimension named above; an argument that names none is the same for every part. Nothing has to cross between parts.
Inputs may be any that keep to these rules, and one draw needn't show every extreme that they name: `counts`: in every expert index some device holds 144 valid rows. send_counts[i, d] = 0 for d the dp index of device i, and a device hands at most counts[i] rows in all; after the moves every device holds at most 96 rows, and in every expert index some device holds exactly 96; in every expert index some entry is exactly 48. `routes`: the 8 ids of a row differ; experts 0 to 3 are held here, expert x on index x of expert, the others lie outside. Among the live rows a device holds after the rebalance, each expert held here is named by 1 to 4 rows, and one of them, the same on every device, by exactly 4 rows on every device.
All inputs are finite; a program needn't handle non-finite values.
Results may differ from a plain program's by a relative error of at most 0.0025.
Values may be sent and summed in bfloat16 or wider, within the bound.
A program may use at most 128 MiB of HBM per device.

v0:
```python
import jax
import jax.numpy as jnp
from jax import lax
from jax.sharding import PartitionSpec as P

BAL = 96
T_MAX = 48
M = 4


EPSILON = 1e-06


def rms_normed(row_block, norm_gain):
    values = row_block.astype(jnp.float32)
    scale_row = lax.rsqrt(jnp.mean(values * values, axis=-1, keepdims=True) + EPSILON)
    return (values * scale_row * norm_gain.astype(jnp.float32)).astype(jnp.bfloat16)


def slot_tables(routes_bal, live_rows, experts_here, capacity):
    expert_ids = jnp.arange(experts_here, dtype=jnp.int32)
    matches = (routes_bal[:, :, None] == expert_ids[None, None, :]) & live_rows[:, None, None]
    is_named = jnp.any(matches, axis=1)
    order_rank = jnp.cumsum(is_named.astype(jnp.int32), axis=0) - 1
    placed = (
        order_rank[:, :, None] == jnp.arange(capacity, dtype=jnp.int32)[None, None, :]
    ) & is_named[:, :, None]
    return (matches, placed)


def combine_matrix(matches, placed, weights_bal):
    weight_each = jnp.sum(weights_bal.astype(jnp.float32)[:, :, None] * matches, axis=1)
    weight_table = weight_each[:, :, None] * placed
    return weight_table.reshape(weight_table.shape[0], -1)


def swiglu_rows(received, gate_weight, up_weight):
    gate_part = jnp.einsum("smd,df->smf", received, gate_weight, preferred_element_type=jnp.float32)
    upward = jnp.einsum("smd,df->smf", received, up_weight, preferred_element_type=jnp.float32)
    return (jax.nn.silu(gate_part) * upward).astype(jnp.bfloat16)


def body(tokens, counts, send_counts, routes, route_weights, norm_gain, w_gate, w_up, w_down):
    dp_size = lax.axis_size("dp")
    expert_size = lax.axis_size("expert")
    model_width = tokens.shape[1]
    top_width = routes.shape[1]
    zero_half = jnp.zeros((), jnp.bfloat16)
    send_row = send_counts[0]
    kept_rows = counts[0] - jnp.sum(send_row)
    out_offset = jnp.cumsum(send_row) - send_row
    place_ids = jnp.arange(T_MAX, dtype=jnp.int32)
    outgoing = place_ids[None, :] < send_row[:, None]
    source_rows = jnp.where(outgoing, kept_rows + out_offset[:, None] + place_ids[None, :], 0)
    out_tokens = jnp.where(outgoing[:, :, None], jnp.take(tokens, source_rows, axis=0), zero_half)
    out_routes = jnp.take(routes, source_rows, axis=0)
    out_weights = jnp.take(route_weights, source_rows, axis=0)
    got_tokens, got_routes, got_weights, got_counts = (
        lax.all_to_all(out_tokens, "dp", split_axis=0, concat_axis=0, tiled=True),
        lax.all_to_all(out_routes, "dp", split_axis=0, concat_axis=0, tiled=True),
        lax.all_to_all(out_weights, "dp", split_axis=0, concat_axis=0, tiled=True),
        lax.all_to_all(send_row[:, None], "dp", split_axis=0, concat_axis=0, tiled=True),
    )
    arrivals = got_counts[:, 0]
    in_offset = (jnp.cumsum(arrivals) - arrivals).astype(jnp.int32)
    position = jnp.arange(BAL, dtype=jnp.int32)
    own_rows = position < kept_rows
    beyond = position - kept_rows
    hit_table = (beyond[:, None] >= in_offset[None, :]) & (
        beyond[:, None] < (in_offset + arrivals)[None, :]
    )
    from_other = jnp.any(hit_table, axis=1)
    source_ids = jnp.arange(dp_size, dtype=jnp.int32)
    flat_index = jnp.sum(
        jnp.where(hit_table, source_ids[None, :] * T_MAX + beyond[:, None] - in_offset[None, :], 0),
        axis=1,
    )
    own_index = jnp.where(own_rows, position, 0)
    live_rows = own_rows | from_other
    arrived_rows = jnp.take(got_tokens.reshape(-1, model_width), flat_index, axis=0)
    moved_rows = jnp.where(
        own_rows[:, None],
        jnp.take(tokens, own_index, axis=0),
        jnp.where(from_other[:, None], arrived_rows, zero_half),
    )
    routes_bal = jnp.where(
        own_rows[:, None],
        jnp.take(routes, own_index, axis=0),
        jnp.take(got_routes.reshape(-1, top_width), flat_index, axis=0),
    )
    weights_bal = jnp.where(
        own_rows[:, None],
        jnp.take(route_weights, own_index, axis=0),
        jnp.take(got_weights.reshape(-1, top_width), flat_index, axis=0),
    )
    normed = rms_normed(moved_rows, norm_gain)
    matches, placed = slot_tables(routes_bal, live_rows, expert_size, M)
    picker = placed.reshape(BAL, -1).T.astype(jnp.bfloat16)
    outbound = (
        jnp.dot(picker, normed, preferred_element_type=jnp.float32)
        .astype(jnp.bfloat16)
        .reshape(expert_size, M, model_width)
    )
    gate_weight = w_gate[0]
    up_weight = w_up[0]
    down_weight = w_down[0]
    replicated = jnp.broadcast_to(
        outbound[:, None], (expert_size, dp_size, M, model_width)
    ).reshape(expert_size * dp_size, M, model_width)
    hidden = swiglu_rows(
        lax.all_to_all(replicated, ("expert", "dp"), split_axis=0, concat_axis=0, tiled=True),
        gate_weight,
        up_weight,
    )
    hidden_ej = hidden.reshape(expert_size, dp_size, M, -1)
    pieces = jnp.einsum(
        "smf,fd->smd",
        hidden_ej.reshape(expert_size * dp_size, M, -1),
        down_weight,
        preferred_element_type=jnp.float32,
    ).astype(jnp.bfloat16)
    returned = lax.all_to_all(pieces, ("expert", "dp"), split_axis=0, concat_axis=0, tiled=True)
    expert_out = jnp.sum(
        returned.reshape(expert_size, dp_size, M, model_width).astype(jnp.float32), axis=1
    ).astype(jnp.bfloat16)
    weight_table = combine_matrix(matches, placed, weights_bal)
    mixed_in = jnp.dot(
        weight_table,
        expert_out.reshape(-1, model_width).astype(jnp.float32),
        precision=lax.Precision.HIGHEST,
    )
    return (moved_rows.astype(jnp.float32) + mixed_in).astype(jnp.bfloat16)


def solution(mesh):
    in_specs = (
        P(("group", "expert", "dp"), None),
        P(("group", "expert", "dp")),
        P(("group", "expert", "dp"), None),
        P(("group", "expert", "dp"), None),
        P(("group", "expert", "dp"), None),
        P(),
        P("expert", None, "dp"),
        P("expert", None, "dp"),
        P("expert", "dp", None),
    )
    out_specs = P(("group", "expert", "dp"), None)
    return jax.shard_map(body, mesh=mesh, in_specs=in_specs, out_specs=out_specs, check_vma=False)
```

profile of v0, /device:TPU:0, one launch (start us, length us, event | category | flops | bytes accessed | tf_op | source)
XLA Modules:
  0.0 184.2 jit_solution(1194371238243063768)
XLA Ops:
  0.0 1.5 copy.74
  1.5 6.3 %all-to-all-start = ((s32[4,1,1]{2,1,0:T(1,128)}), s32[4,1,1]{2,1,0:T(1,128)S(1)}, u32[]{:S(2)}, u32[]{:S(2)}) async-start(s32[4,1,1]{2,1,0:T(1,128)} %copy.74), calls=%async_computation | async-start | bytes 4096 | tf_op jit(solution)/shard_map/all_to_all | solution.py:62
  7.8 1.4 reduce_sum.50
  9.2 0.8 reduce-window.16
  11.3 0.7 fusion.44
  12.0 0.7 compare_select_fusion
  12.7 0.7 iota_compare_fusion.3
  13.5 0.1 reshape.404
  13.6 0.8 copy.75
  14.4 3.9 %gather_fusion.1 = bf16[192,7168]{1,0:T(8,128)(2,1)} fusion(bf16[144,7168]{1,0:T(8,128)(2,1)S(1)} %copy-done, s32[1024]{0:T(1024)S(1)} %pad_clamp_fusion.1), kind=kCustom, calls=%fused_computation.1 | custom fusion | bytes 5505792 | tf_op jit(solution)/shard_map/jit(_take)/gather | solution.py:55
  18.2 0.7 gather_fusion.4
  19.0 0.7 reshape.475
  19.7 5.1 %all-to-all-start.2 = ((s32[4,1,384]{2,1,0:T(1,128)}), s32[4,1,384]{2,1,0:T(1,128)S(1)}, u32[]{:S(2)}, u32[]{:S(2)}) async-start(s32[4,1,384]{2,1,0:T(1,128)} %reshape.475), calls=%async_computation.2 | async-start | bytes 12288 | tf_op jit(solution)/shard_map/all_to_all | solution.py:60
  24.8 3.7 %select_select_fusion = bf16[4,48,7168]{2,1,0:T(8,128)(2,1)} fusion(bf16[4,48,7168]{2,1,0:T(8,128)(2,1)} %bitcast.63, pred[4,48]{1,0:T(4,128)(4,1)S(1)} %get-tuple-element.8, pred[4,48]{1,0:T(4,128)(4,1)S(1)} %get-tuple-element.7), kind=kLoop, calls=%fused_computation.24 | loop fusion | flops 2752512 | bytes 5505408 | tf_op jit(solution)/shard_map/jit(_where)/select_n | solution.py:55
  28.5 1.9 %all-to-all-done.2 = s32[4,1,384]{2,1,0:T(1,128)S(1)} async-done(((s32[4,1,384]{2,1,0:T(1,128)}), s32[4,1,384]{2,1,0:T(1,128)S(1)}, u32[]{:S(2)}, u32[]{:S(2)}) %all-to-all-start.2) | async-done | bytes 6176 | tf_op jit(solution)/shard_map/all_to_all | solution.py:60
  30.4 4.6 %all-to-all-start.1 = ((bf16[4,48,7168]{2,1,0:T(8,128)(2,1)}), bf16[4,48,7168]{2,1,0:T(8,128)(2,1)}, u32[]{:S(2)}, u32[]{:S(2)}) async-start(bf16[4,48,7168]{2,1,0:T(8,128)(2,1)} %select_select_fusion), calls=%async_computation.1 | async-start | bytes 5505024 | tf_op jit(solution)/shard_map/all_to_all | solution.py:59
  35.0 1.4 gather_fusion
  36.4 1.2 gather_fusion.3
  37.6 0.6 convert_element_type.45
  38.3 1.5 copy.76
  39.7 0.7 eq.45
  40.4 0.6 select_compare_fusion
  41.0 0.2 reduce.2
  41.1 0.2 reduce-window.15
  41.3 0.1 select_reduce_fusion.1
  41.4 0.6 pad_clamp_fusion
  42.0 0.1 fusion.47
  42.1 0.5 compare_and_fusion.1
  42.7 0.5 fusion.48
  43.2 0.5 broadcast.338
  43.7 0.7 reduce.4
  44.4 0.1 reshape.476
  44.4 0.1 copy.79
  44.5 1.3 gather_fusion.5
  45.9 0.9 copy.80
  46.7 0.7 select_select_fusion.2
  47.4 0.6 fusion.31
  48.1 0.1 copy.81
  48.2 0.1 reduce_window_sum.20
  48.4 47.1 %all-to-all-done.1 = bf16[4,48,7168]{2,1,0:T(8,128)(2,1)} async-done(((bf16[4,48,7168]{2,1,0:T(8,128)(2,1)}), bf16[4,48,7168]{2,1,0:T(8,128)(2,1)}, u32[]{:S(2)}, u32[]{:S(2)}) %all-to-all-start.1) | async-done | bytes 2752544 | tf_op jit(solution)/shard_map/all_to_all | solution.py:59
  95.6 6.0 %gather_fusion.2 = bf16[96,7168]{1,0:T(8,128)(2,1)} fusion(bf16[192,7168]{1,0:T(8,128)(2,1)} %bitcast.8, s32[1024]{0:T(1024)} %pad_clamp_fusion), kind=kCustom, calls=%fused_computation.2 | custom fusion | bytes 2752896 | tf_op jit(solution)/shard_map/jit(_take)/gather | solution.py:80
  101.6 2.7 %fusion.7 = (f32[96]{0:T(128)S(1)}, bf16[96,7168]{1,0:T(8,128)(2,1)S(1)}) fusion(bf16[96,7168]{1,0:T(8,128)(2,1)} %gather_fusion.2, pred[96]{0:T(512)(128)(4,1)S(1)} %copy-done.11, pred[96]{0:T(512)(128)(4,1)S(1)} %copy-done.15, bf16[96,7168]{1,0:T(8,128)(2,1)S(1)} %gather_fusion, pred[96]{0:T(512)(128)(4,1)S(1)} %copy-done.9, pred[96]{0:T(512)(128)(4,1)S(1)} %copy-done.10), kind=kLoop, calls=%fused_computation.21 | loop fusion | flops 4816800 | bytes 4129536 | tf_op jit(solution)/shard_map/reduce_sum | solution.py:16
  104.4 1.0 copy-done.1
  105.4 0.5 convolution_convert_fusion.1
  106.0 0.1 broadcast_in_dim.195
  106.1 1.2 broadcast_in_dim.196
  107.2 3.8 %all-to-all-start.4 = ((bf16[16,4,7168]{2,1,0:T(4,128)(2,1)}), bf16[16,4,7168]{2,1,0:T(4,128)(2,1)S(1)}, u32[]{:S(2)}, u32[]{:S(2)}) async-start(bf16[16,4,7168]{2,1,0:T(4,128)(2,1)} %bitcast.64), calls=%async_computation.4 | async-start | bytes 1835008 | tf_op jit(solution)/shard_map/all_to_all | solution.py:111
  111.1 0.1 copy.83
  111.2 0.8 gather_fusion.7
  112.0 0.1 copy.86
  112.1 0.7 reshape.477
  112.7 22.5 %all-to-all-done.4 = bf16[16,4,7168]{2,1,0:T(4,128)(2,1)S(1)} async-done(((bf16[16,4,7168]{2,1,0:T(4,128)(2,1)}), bf16[16,4,7168]{2,1,0:T(4,128)(2,1)S(1)}, u32[]{:S(2)}, u32[]{:S(2)}) %all-to-all-start.4) | async-done | bytes 917536 | tf_op jit(solution)/shard_map/all_to_all | solution.py:111
  135.2 3.4 %all-to-all-start.3 = ((bf16[4,2,192]{2,1,0:T(2,128)(2,1)}), bf16[4,2,192]{2,1,0:T(2,128)(2,1)S(1)}, u32[]{:S(2)}, u32[]{:S(2)}) async-start(bf16[4,2,192]{2,1,0:T(2,128)(2,1)} %reshape.477), calls=%async_computation.3 | async-start | bytes 8192 | tf_op jit(solution)/shard_map/all_to_all | solution.py:61
  138.6 2.8 %fusion.5 = f32[16,4,256]{2,0,1:T(8,128)S(1)} fusion(bf16[1,7168,256]{2,1,0:T(8,128)(2,1)} %param.15, bf16[16,4,7168]{2,1,0:T(4,128)(2,1)S(1)} %all-to-all-done.4), kind=kOutput, calls=%fused_computation.19 | convolution fusion | flops 234881024 | bytes 4653056 | tf_op jit(solution)/shard_map/smd,df->smf/dot_general | solution.py:38
  141.4 6.4 %convolution_convert_fusion = bf16[16,4,7168]{2,0,1:T(8,128)(2,1)} fusion(bf16[1,256,7168]{2,1,0:T(8,128)(2,1)} %param.17, bf16[1,7168,256]{2,1,0:T(8,128)(2,1)} %param.16, bf16[16,4,7168]{2,1,0:T(4,128)(2,1)S(1)} %all-to-all-done.4, f32[16,4,256]{2,0,1:T(8,128)S(1)} %fusion.5), kind=kOutput, calls=%fused_computation.12 | convolution fusion | flops 470319104 | bytes 9240576 | tf_op jit(solution)/shard_map/smf,fd->smd/dot_general | solution.py:116
  147.9 2.8 %copy.91 = bf16[16,4,7168]{2,1,0:T(4,128)(2,1)} copy(bf16[16,4,7168]{2,0,1:T(8,128)(2,1)} %convolution_convert_fusion) | data formatting | bytes 1835008 | tf_op jit(solution)/shard_map/convert_element_type | solution.py:121
  150.7 5.0 %all-to-all-start.5 = ((bf16[16,4,7168]{2,1,0:T(4,128)(2,1)}), bf16[16,4,7168]{2,1,0:T(4,128)(2,1)S(1)}, u32[]{:S(2)}, u32[]{:S(2)}) async-start(bf16[16,4,7168]{2,1,0:T(4,128)(2,1)} %copy.91), calls=%async_computation.5 | async-start | bytes 1835008 | tf_op jit(solution)/shard_map/all_to_all | solution.py:122
  155.7 0.8 gather_fusion.6
  156.6 0.1 reshape.478
  156.7 0.1 copy.87
  156.8 0.8 gather_fusion.8
  157.7 22.2 %all-to-all-done.5 = bf16[16,4,7168]{2,1,0:T(4,128)(2,1)S(1)} async-done(((bf16[16,4,7168]{2,1,0:T(4,128)(2,1)}), bf16[16,4,7168]{2,1,0:T(4,128)(2,1)S(1)}, u32[]{:S(2)}, u32[]{:S(2)}) %all-to-all-start.5) | async-done | bytes 917536 | tf_op jit(solution)/shard_map/all_to_all | solution.py:122
  179.9 0.5 bitcast_reduce_fusion
  180.3 3.8 %fusion.1 = bf16[96,7168]{1,0:T(8,128)(2,1)} fusion(bf16[4,4,7168]{2,1,0:T(4,128)(2,1)S(1)} %bitcast_reduce_fusion, bf16[96,7168]{1,0:T(8,128)(2,1)} %copy-done.1, f32[96,4]{0,1:T(4,128)S(1)} %select_reduce_fusion, s32[96,4]{0,1:T(4,128)S(1)} %copy.82, pred[96,4]{0,1:T(4,128)(4,1)S(1)} %fusion.31), kind=kOutput, calls=%fused_computation.11 | convolution fusion | flops 134189568 | bytes 2985344 | tf_op jit(solution)/shard_map/dot_general | solution.py:127
  (56 shorter events, 0.5 us)
Async XLA Ops:
  0.0 14.4 %copy-start = (bf16[144,7168]{1,0:T(8,128)(2,1)S(1)}, bf16[144,7168]{1,0:T(8,128)(2,1)}, u32[]{:S(2)}) copy-start(bf16[144,7168]{1,0:T(8,128)(2,1)} %param.9) | copy-start | bytes 6193156
  1.5 18.2 %all-to-all-start = ((s32[4,1,1]{2,1,0:T(1,128)}), s32[4,1,1]{2,1,0:T(1,128)S(1)}, u32[]{:S(2)}, u32[]{:S(2)}) async-start(s32[4,1,1]{2,1,0:T(1,128)} %copy.74), calls=%async_computation | async-start | bytes 4096 | tf_op jit(solution)/shard_map/all_to_all | solution.py:62
  13.5 11.3 %copy-start.6 = (pred[4,48]{1,0:T(4,128)(4,1)}, pred[4,48]{1,0:T(4,128)(4,1)S(1)}, u32[]{:S(2)}) copy-start(pred[4,48]{1,0:T(4,128)(4,1)S(1)} %get-tuple-element.8) | copy-start | bytes 580
  13.6 4.7 %copy-start.3 = (s32[1024]{0:T(1024)}, s32[1024]{0:T(1024)S(1)}, u32[]{:S(2)}) copy-start(s32[1024]{0:T(1024)S(1)} %pad_clamp_fusion.1) | copy-start | bytes 12292
  19.7 10.7 %all-to-all-start.2 = ((s32[4,1,384]{2,1,0:T(1,128)}), s32[4,1,384]{2,1,0:T(1,128)S(1)}, u32[]{:S(2)}, u32[]{:S(2)}) async-start(s32[4,1,384]{2,1,0:T(1,128)} %reshape.475), calls=%async_computation.2 | async-start | bytes 12288 | tf_op jit(solution)/shard_map/all_to_all | solution.py:60
  30.4 65.2 %all-to-all-start.1 = ((bf16[4,48,7168]{2,1,0:T(8,128)(2,1)}), bf16[4,48,7168]{2,1,0:T(8,128)(2,1)}, u32[]{:S(2)}, u32[]{:S(2)}) async-start(bf16[4,48,7168]{2,1,0:T(8,128)(2,1)} %select_select_fusion), calls=%async_computation.1 | async-start | bytes 5505024 | tf_op jit(solution)/shard_map/all_to_all | solution.py:59
  35.0 1.4 copy-start.8
  35.0 2.7 %copy-start.5 = (bf16[7168]{0:T(1024)(128)(2,1)S(1)}, bf16[7168]{0:T(1024)(128)(2,1)}, u32[]{:S(2)}) copy-start(bf16[7168]{0:T(1024)(128)(2,1)} %param.14) | copy-start | bytes 43012
  42.1 2.3 %copy-start.14 = (pred[96]{0:T(512)(128)(4,1)}, pred[96]{0:T(512)(128)(4,1)S(1)}, u32[]{:S(2)}) copy-start(pred[96]{0:T(512)(128)(4,1)S(1)} %fusion.47) | copy-start | bytes 292
  95.5 6.0 %copy-start.9 = (pred[96]{0:T(512)(128)(4,1)S(1)}, pred[96]{0:T(512)(128)(4,1)}, u32[]{:S(2)}) copy-start(pred[96]{0:T(512)(128)(4,1)} %get-tuple-element.9) | copy-start | bytes 292
  95.5 6.0 %copy-start.10 = (pred[96]{0:T(512)(128)(4,1)S(1)}, pred[96]{0:T(512)(128)(4,1)}, u32[]{:S(2)}) copy-start(pred[96]{0:T(512)(128)(4,1)} %get-tuple-element.10) | copy-start | bytes 292
  95.5 6.0 %copy-start.11 = (pred[96]{0:T(512)(128)(4,1)S(1)}, pred[96]{0:T(512)(128)(4,1)}, u32[]{:S(2)}) copy-start(pred[96]{0:T(512)(128)(4,1)} %compare_and_fusion.1) | copy-start | bytes 292
  95.5 6.0 %copy-start.15 = (pred[96]{0:T(512)(128)(4,1)S(1)}, pred[96]{0:T(512)(128)(4,1)}, u32[]{:S(2)}) copy-start(pred[96]{0:T(512)(128)(4,1)} %copy-done.14) | copy-start | bytes 292
  101.6 3.9 %copy-start.2 = (f32[7168]{0:T(1024)S(1)}, f32[7168]{0:T(1024)}, u32[]{:S(2)}) copy-start(f32[7168]{0:T(1024)} %convert_element_type.45) | copy-start | bytes 86020
  101.6 3.9 %copy-start.16 = (s32[16]{0:T(128)S(1)}, s32[16]{0:T(128)}, u32[]{:S(2)}) copy-start(s32[16]{0:T(128)} %eq.45) | copy-start | bytes 196
  104.3 1.1 copy-start.1
  105.4 5.6 %copy-start.12 = (bf16[144,8]{0,1:T(8,128)(2,1)S(1)}, bf16[144,8]{0,1:T(8,128)(2,1)}, u32[]{:S(2)}) copy-start(bf16[144,8]{0,1:T(8,128)(2,1)} %param.13) | copy-start | bytes 6916
  105.4 5.7 %copy-start.4 = (s32[1024]{0:T(1024)S(1)}, s32[1024]{0:T(1024)}, u32[]{:S(2)}) copy-start(s32[1024]{0:T(1024)} %copy-done.3) | copy-start | bytes 12292
  105.4 6.6 %copy-start.7 = (pred[4,48]{1,0:T(4,128)(4,1)S(1)}, pred[4,48]{1,0:T(4,128)(4,1)}, u32[]{:S(2)}) copy-start(pred[4,48]{1,0:T(4,128)(4,1)} %copy-done.6) | copy-start | bytes 580
  107.2 28.0 %all-to-all-start.4 = ((bf16[16,4,7168]{2,1,0:T(4,128)(2,1)}), bf16[16,4,7168]{2,1,0:T(4,128)(2,1)S(1)}, u32[]{:S(2)}, u32[]{:S(2)}) async-start(bf16[16,4,7168]{2,1,0:T(4,128)(2,1)} %bitcast.64), calls=%async_computation.4 | async-start | bytes 1835008 | tf_op jit(solution)/shard_map/all_to_all | solution.py:111
  135.2 15.5 %all-to-all-start.3 = ((bf16[4,2,192]{2,1,0:T(2,128)(2,1)}), bf16[4,2,192]{2,1,0:T(2,128)(2,1)S(1)}, u32[]{:S(2)}, u32[]{:S(2)}) async-start(bf16[4,2,192]{2,1,0:T(2,128)(2,1)} %reshape.477), calls=%async_computation.3 | async-start | bytes 8192 | tf_op jit(solution)/shard_map/all_to_all | solution.py:61
  147.9 9.8 %copy-start.13 = (pred[96]{0:T(512)(128)(4,1)S(1)}, pred[96]{0:T(512)(128)(4,1)}, u32[]{:S(2)}) copy-start(pred[96]{0:T(512)(128)(4,1)} %fusion.48) | copy-start | bytes 292
  150.7 29.2 %all-to-all-start.5 = ((bf16[16,4,7168]{2,1,0:T(4,128)(2,1)}), bf16[16,4,7168]{2,1,0:T(4,128)(2,1)S(1)}, u32[]{:S(2)}, u32[]{:S(2)}) async-start(bf16[16,4,7168]{2,1,0:T(4,128)(2,1)} %copy.91), calls=%async_computation.5 | async-start | bytes 1835008 | tf_op jit(solution)/shard_map/all_to_all | solution.py:122
where the time goes:
time: 185 us; the launch traced here: 184 us
  waiting for transfers between devices  93.6 us (51%)
  local copies, waits for them, and re-layouts  30.3 us (16%)
  starting transfers between devices  28.2 us (15%)
  other arithmetic  16.8 us (9%)
  matrix products  13.6 us (7%)
    all_to_all x1, waiting for transfers between devices, body(): lax.all_to_all(out_tokens, 'dp', split_axis=0, concat_axis=0, tiled=True)  47.1 us
    all_to_all x1, waiting for transfers between devices, body(): lax.all_to_all(replicated, ('expert', 'dp'), split_axis=0, concat_axis=0,...  22.5 us
    all_to_all x1, waiting for transfers between devices, body(): lax.all_to_all(pieces, ('expert', 'dp'), split_axis=0, concat_axis=0, til...  22.2 us
    dot_general x1, matrix products, body(): jnp.einsum('smf,fd->smd', hidden_ej.reshape(expert_size * dp_size, M, -1)...  6.44 us
    all_to_all x1, starting transfers between devices, body(): lax.all_to_all(send_row[:, None], 'dp', split_axis=0, concat_axis=0, tile...  6.32 us
    gather x1, local copies, waits for them, and re-layouts, body(): jnp.take(got_tokens.reshape(-1, model_width), flat_index, axis=0)  6 us
    all_to_all x1, starting transfers between devices, body(): lax.all_to_all(out_routes, 'dp', split_axis=0, concat_axis=0, tiled=True)  5.09 us
    all_to_all x1, starting transfers between devices, body(): lax.all_to_all(pieces, ('expert', 'dp'), split_axis=0, concat_axis=0, til...  5 us
  transfers between devices with their start and end apart: 6, of which 4 were waited for; matrix products, arithmetic and copies ran while one was open for 24% of the time, Pallas kernels for 0%

commit v1 on v0

v1 whole, which is shorter than its diff:
```python
import functools
import jax
import jax.numpy as jnp
from jax import lax
from jax.experimental import pallas as pl
from jax.experimental.pallas import tpu as pltpu
from jax.sharding import PartitionSpec as P

BAL = 96
T_MAX = 48
M = 4
EPSILON = 1e-06
LANES = 128
CHUNK = 1024
MESH = pl.DeviceIdType.MESH
BF = jnp.bfloat16
F32 = jnp.float32


def dot(a, b):
    return jnp.dot(a.astype(BF), b.astype(BF), preferred_element_type=F32)


def dot_nt(a, b):
    return lax.dot_general(
        a.astype(BF), b.astype(BF), (((1,), (1,)), ((), ())), preferred_element_type=F32
    )


def iota(shape, dim):
    return lax.broadcasted_iota(jnp.int32, shape, dim).astype(F32)


def kernel(n_e, n_d, tokens, fields, plan, gain, wg_hbm, wu_hbm, wd_hbm, out,
           wg, wu, wd, meta_out, meta_in, rows_out, rest_out, rows_in, rest_in,
           acc, wide, send1, recv1, recv2, recv3, send4, recv4, gate, up,
           w_sem, meta_s, meta_r, rows_s, rows_r, rest_s, rest_r,
           s1, r1, s2, r2, s3, r3, s4, r4):
    e, d = lax.axis_index("expert"), lax.axis_index("dp")
    width = tokens.shape[1]
    cap = tokens.shape[0]
    slots = n_e * M
    first = rows_out.shape[1]
    rest = T_MAX - first
    chunks = width // CHUNK
    dps = [lax.rem(d + k, n_d) for k in range(1, n_d)]
    exs = [lax.rem(e + k, n_e) for k in range(1, n_e)]

    def each_chunk(fn):
        def step(c, carry):
            fn(pl.ds(pl.multiple_of(c * CHUNK, CHUNK), CHUNK))
            return carry
        lax.fori_loop(0, chunks, step, 0)

    def remote(src, dst, send, recv, device):
        return pltpu.make_async_remote_copy(
            src_ref=src, dst_ref=dst, send_sem=send, recv_sem=recv,
            device_id=device, device_id_type=MESH)

    loads = [pltpu.make_async_copy(a, b, w_sem.at[i])
             for i, (a, b) in enumerate(((wg_hbm, wg), (wu_hbm, wu), (wd_hbm, wd)))]
    for copy in loads:
        copy.start()

    barrier = pltpu.get_barrier_semaphore()
    for j in dps:
        pl.semaphore_signal(barrier, inc=1, device_id={"dp": j}, device_id_type=MESH)
    for x in exs:
        pl.semaphore_signal(barrier, inc=1, device_id={"expert": x}, device_id_type=MESH)

    lanes = plan.shape[1]
    upper = (iota((lanes, lanes), 0) < iota((lanes, lanes), 1)).astype(BF)
    target, named = plan[0:1, :], plan[1:2, :]
    picks = []
    for k, j in enumerate(dps):
        mine = (target == j.astype(F32)).astype(F32)
        ahead = mine * named
        behind = mine - ahead
        before_a = dot(jnp.broadcast_to(ahead, (8, lanes)), upper)[0:1]
        before_b = dot(jnp.broadcast_to(behind, (8, lanes)), upper)[0:1]
        total = jnp.sum(ahead, axis=1, keepdims=True)
        slot = jnp.where(ahead > 0, before_a, jnp.where(behind > 0, total + before_b, -1.0))
        pick = (iota((LANES, lanes), 0) == slot).astype(F32)
        meta_out[k] = dot_nt(fields[...], pick)
        picks.append(pick.astype(BF)[:T_MAX, :cap])

    pl.semaphore_wait(barrier, n_d - 1 + n_e - 1)
    meta_copies, row_copies, rest_copies = [], [], []
    for k, j in enumerate(dps):
        def pack(cols, k=k):
            block = dot(picks[k], tokens[:, cols]).astype(BF)
            rows_out[k, :, cols] = block[:first]
            if rest:
                rest_out[k, :, cols] = block[first:]
        copy = remote(meta_out.at[k], meta_in.at[d], meta_s.at[k], meta_r.at[d], {"dp": j})
        copy.start()
        meta_copies.append(copy)
        each_chunk(pack)
        copy = remote(rows_out.at[k], rows_in.at[d], rows_s.at[k], rows_r.at[d], {"dp": j})
        copy.start()
        row_copies.append(copy)

    def arrival(src, buf, sems, j, axis="dp"):
        return remote(src, buf.at[j], sems.at[j], sems.at[j], {axis: j})

    own = (target == -1.0).astype(F32)
    kept = jnp.sum(own, axis=1, keepdims=True)
    own_f = fields[...] * own
    rank_of = lax.broadcasted_iota(jnp.int32, (slots, 1), 0) % M
    rank_of = rank_of.astype(F32)
    base = jnp.zeros((slots, 1), F32)

    def place(weights, base, tri):
        has = (weights > 0).astype(F32)
        rank = dot(has, tri) + base
        placed = has * (rank == rank_of).astype(F32)
        return placed, base + jnp.sum(has, axis=1, keepdims=True)

    placed, base = place(own_f[:slots], base, upper)
    seat = jnp.where(own > 0, iota((1, lanes), 1), -1.0)
    a_own = (iota((BAL, lanes), 0) == seat).astype(F32)
    table = dot_nt(a_own, placed * own_f[:slots])
    a_own = a_own.astype(BF)[:, :cap]
    p_own = placed.astype(BF)[:, :cap]

    def own_part(cols):
        block = tokens[:, cols]
        acc[:, cols] = dot(a_own, block)
        wide[:, cols] = dot(p_own, block)
    each_chunk(own_part)

    meta_in[d] = jnp.zeros(meta_in.shape[1:], F32)
    for k, j in enumerate(dps):
        arrival(meta_out.at[k], meta_in, meta_r, j).wait_recv()
    tri = upper[:LANES, :LANES]
    offset = kept
    seats, places = [], []
    for j in range(n_d):
        f = meta_in[j]
        placed, base = place(f[:slots], base, tri)
        valid = f[slots:slots + 1]
        seat = jnp.where(valid > 0, f[slots + 1:slots + 2] + offset, -1.0)
        offset = offset + jnp.sum(valid, axis=1, keepdims=True)
        a = (iota((BAL, LANES), 0) == seat).astype(F32)
        table = table + dot_nt(a, placed * f[:slots])
        seats.append(a.astype(BF)[:, :T_MAX])
        places.append(placed.astype(BF)[:, :first])

    rows_in[d] = jnp.zeros(rows_in.shape[1:], BF)
    for k, j in enumerate(dps):
        arrival(rows_out.at[k], rows_in, rows_r, j).wait_recv()

    def named_part(cols):
        total = wide[:, cols]
        for j in range(n_d):
            total = total + dot(places[j], rows_in[j, :, cols])
        wide[:, cols] = total
    each_chunk(named_part)

    def squares(c, carry):
        v = wide[:, pl.ds(pl.multiple_of(c * CHUNK, CHUNK), CHUNK)]
        return carry + jnp.sum(v * v, axis=1, keepdims=True)
    scale = lax.rsqrt(lax.fori_loop(0, chunks, squares, jnp.zeros((slots, 1), F32)) / width + EPSILON)

    def norm(cols):
        wide[:, cols] = wide[:, cols] * scale * gain[:, cols]
        for x in range(n_e):
            send1[x, :, cols] = wide[x * M:(x + 1) * M, cols].astype(BF)
    each_chunk(norm)

    one_copies = []
    for k, x in enumerate(exs):
        copy = remote(send1.at[x], recv1.at[e], s1.at[k], r1.at[e], {"expert": x})
        copy.start()
        one_copies.append(copy)
    recv1[e] = send1[e]
    for k, x in enumerate(exs):
        arrival(send1.at[x], recv1, r1, x, "expert").wait_recv()

    def gather(cols):
        for x in range(n_e):
            wide[x * M:(x + 1) * M, cols] = recv1[x, :, cols].astype(F32)
        recv2[d, :, cols] = wide[:, cols].astype(BF)
    each_chunk(gather)

    two_copies = []
    for k, j in enumerate(dps):
        copy = remote(recv2.at[d], recv2.at[d], s2.at[k], r2.at[d], {"dp": j})
        copy.start()
        two_copies.append(copy)
    if rest:
        for k, j in enumerate(dps):
            copy = remote(rest_out.at[k], rest_in.at[d], rest_s.at[k], rest_r.at[d], {"dp": j})
            copy.start()
            rest_copies.append(copy)

    def got_part(cols):
        total = acc[:, cols]
        for j in range(n_d):
            total = total + dot(seats[j][:, :first], rows_in[j, :, cols])
        acc[:, cols] = total
    each_chunk(got_part)
    for copy in loads:
        copy.wait()
    for k, j in enumerate(dps):
        arrival(recv2.at[d], recv2, r2, j).wait_recv()

    gate[...] = jnp.zeros_like(gate)
    up[...] = jnp.zeros_like(up)

    def project(cols):
        x = recv2[:, :, cols].reshape(n_d * slots, CHUNK)
        gate[...] += dot(x, wg[cols, :])
        up[...] += dot(x, wu[cols, :])
    each_chunk(project)
    g = gate[...]
    hidden = (g / (1.0 + jnp.exp(-g)) * up[...]).astype(BF)
    for copy in two_copies:
        copy.wait_send()

    def down(cols):
        piece = dot(hidden, wd[:, cols]).astype(BF)
        recv2[:, :, cols] = piece.reshape(n_d, slots, CHUNK)
    each_chunk(down)
    three_copies = []
    for k, j in enumerate(dps):
        copy = remote(recv2.at[j], recv3.at[d], s3.at[k], r3.at[d], {"dp": j})
        copy.start()
        three_copies.append(copy)
    for k, j in enumerate(dps):
        arrival(recv2.at[j], recv3, r3, j).wait_recv()

    def reduce(cols):
        total = recv2[d, :, cols].astype(F32)
        for j in dps:
            total = total + recv3[j, :, cols].astype(F32)
        wide[:, cols] = total
        for x in range(n_e):
            send4[x, :, cols] = wide[x * M:(x + 1) * M, cols].astype(BF)
    each_chunk(reduce)

    four_copies = []
    for k, x in enumerate(exs):
        copy = remote(send4.at[x], recv4.at[e], s4.at[k], r4.at[e], {"expert": x})
        copy.start()
        four_copies.append(copy)
    recv4[e] = send4[e]

    if rest:
        rest_in[d] = jnp.zeros(rest_in.shape[1:], BF)
        for k, j in enumerate(dps):
            arrival(rest_out.at[k], rest_in, rest_r, j).wait_recv()

        def rest_part(cols):
            total = acc[:, cols]
            for j in range(n_d):
                total = total + dot(seats[j][:, first:], rest_in[j, :, cols])
            acc[:, cols] = total
        each_chunk(rest_part)
    for k, x in enumerate(exs):
        arrival(send4.at[x], recv4, r4, x, "expert").wait_recv()
    table = table.astype(BF)

    def finish(cols):
        for x in range(n_e):
            wide[x * M:(x + 1) * M, cols] = recv4[x, :, cols].astype(F32)
        out[:, cols] = (acc[:, cols] + dot(table, wide[:, cols])).astype(BF)
    each_chunk(finish)
    for copy in meta_copies + row_copies + rest_copies + one_copies + three_copies + four_copies:
        copy.wait_send()


def body(tokens, counts, send_counts, routes, route_weights, norm_gain, w_gate, w_up, w_down):
    n_e, n_d = lax.axis_size("expert"), lax.axis_size("dp")
    cap, width = tokens.shape
    part = w_gate.shape[2]
    slots = n_e * M
    first = min(T_MAX, slots)
    rest = T_MAX - first
    lanes = -(-cap // LANES) * LANES
    pad = ((0, 0), (0, lanes - cap))
    ids = jnp.pad(routes.T, pad, constant_values=-1)
    weights = jnp.pad(route_weights.T.astype(F32), pad)
    place = jnp.arange(lanes, dtype=jnp.int32)
    send_row = send_counts[0]
    begin = counts[0] - jnp.sum(send_row)
    target = jnp.where(place < begin, -1, -2)
    index = place
    for j in range(n_d):
        inside = (place >= begin) & (place < begin + send_row[j])
        target = jnp.where(inside, j, target)
        index = jnp.where(inside, place - begin, index)
        begin = begin + send_row[j]
    valid = (target > -2).astype(F32)
    chosen = jnp.stack(
        [jnp.sum(jnp.where(ids == x, weights, 0.0), axis=0) for x in range(n_e)]) * valid
    named = jnp.any(chosen > 0, axis=0).astype(F32)
    height = -(-(slots + 2) // 8) * 8
    fields = jnp.concatenate([
        jnp.repeat(chosen, M, axis=0), valid[None], index.astype(F32)[None],
        jnp.zeros((height - slots - 2, lanes), F32)])
    plan = jnp.concatenate([target.astype(F32)[None], named[None], jnp.zeros((6, lanes), F32)])
    gain = norm_gain.astype(F32)[None]

    vmem = pl.BlockSpec(memory_space=pltpu.VMEM)
    hbm = pl.BlockSpec(memory_space=pl.ANY)
    dma = pltpu.SemaphoreType.DMA
    return pl.pallas_call(
        functools.partial(kernel, n_e, n_d),
        out_shape=jax.ShapeDtypeStruct((BAL, width), BF),
        in_specs=[vmem] * 4 + [hbm] * 3,
        out_specs=vmem,
        scratch_shapes=[
            pltpu.VMEM((width, part), BF),
            pltpu.VMEM((width, part), BF),
            pltpu.VMEM((part, width), BF),
            pltpu.VMEM((n_d - 1, height, LANES), F32),
            pltpu.VMEM((n_d, height, LANES), F32),
            pltpu.VMEM((n_d - 1, first, width), BF),
            pltpu.VMEM((n_d - 1, max(rest, 16), width if rest else LANES), BF),
            pltpu.VMEM((n_d, first, width), BF),
            pltpu.VMEM((n_d, max(rest, 16), width if rest else LANES), BF),
            pltpu.VMEM((BAL, width), F32),
            pltpu.VMEM((slots, width), F32),
            pltpu.VMEM((n_e, M, width), BF),
            pltpu.VMEM((n_e, M, width), BF),
            pltpu.VMEM((n_d, slots, width), BF),
            pltpu.VMEM((n_d, slots, width), BF),
            pltpu.VMEM((n_e, M, width), BF),
            pltpu.VMEM((n_e, M, width), BF),
            pltpu.VMEM((n_d * slots, part), F32),
            pltpu.VMEM((n_d * slots, part), F32),
            dma((3,)),
            dma((n_d,)), dma((n_d,)),
            dma((n_d,)), dma((n_d,)),
            dma((n_d,)), dma((n_d,)),
            dma((n_e,)), dma((n_e,)),
            dma((n_d,)), dma((n_d,)),
            dma((n_d,)), dma((n_d,)),
            dma((n_e,)), dma((n_e,)),
        ],
        compiler_params=pltpu.CompilerParams(
            collective_id=0, has_side_effects=True, vmem_limit_bytes=60 * 1024 * 1024),
    )(tokens, fields, plan, gain, w_gate[0], w_up[0], w_down[0])


def solution(mesh):
    rows = P(("group", "expert", "dp"), None)
    in_specs = (
        rows,
        P(("group", "expert", "dp")),
        rows,
        rows,
        rows,
        P(),
        P("expert", None, "dp"),
        P("expert", None, "dp"),
        P("expert", "dp", None),
    )
    return jax.shard_map(body, mesh=mesh, in_specs=in_specs, out_specs=rows, check_vma=False)
```

time: 185 us -> 135 us (0.73)
  the two profiles are of different devices: /device:TPU:0 before, /device:TPU:27 now
where the time goes in v1:
time: 135 us
  Pallas kernels  122 us (90%)
  other arithmetic  4.72 us (3%)
  local copies, waits for them, and re-layouts  3.99 us (3%)
  between operations  3.93 us (3%)
    pallas_call x1, Pallas kernels, body(): pl.pallas_call(functools.partial(kernel, n_e, n_d), out_shape=jax.ShapeDt...  122 us

profile of v1, /device:TPU:27, one launch (start us, length us, event | category | flops | bytes accessed | tf_op | source)
XLA Modules:
  0.0 134.7 jit_solution(12355294605226704785)
XLA Ops:
  0.7 1.4 %reduce_sum.49 = s32[]{:T(128)} reduce(s32[1,4]{1,0:T(1,128)} %param.11, s32[]{:T(128)} %constant.10.clone.1), dimensions={0,1}, to_apply=%region_4.5 | reduce | flops 3 | bytes 24 | tf_op jit(solution)/shard_map/reduce_sum | solution.py:286
  2.7 1.5 %fusion.7 = (s32[1,1]{1,0:T(1,128)}, s32[1,1]{1,0:T(1,128)}, s32[1,1]{1,0:T(1,128)}, s32[1,1]{1,0:T(1,128)}) fusion(s32[1,4]{1,0:T(1,128)} %param.11), kind=kLoop, calls=%fused_computation.29 | loop fusion | bytes 32 | tf_op jit(solution)/shard_map/slice | solution.py:290
  6.8 0.7 fusion
  7.6 0.6 pad_maximum_fusion.1.plan
  8.2 0.6 pad_maximum_fusion.fields
  8.8 1.3 broadcast_in_dim.69
  10.1 122.0 %shard_map.91 = bf16[96,7168]{1,0:T(8,128)(2,1)} custom-call(bf16[144,7168]{1,0:T(8,128)(2,1)} %tokens.1, f32[24,256]{1,0:T(8,128)} %pad_maximum_fusion.fields, f32[8,256]{1,0:T(8,128)} %pad_maximum_fusion.1.plan, f32[1,7168]{1,0:T(1,128)} %bitcast.20, bf16[7168,256]{1,0:T(8,128)(2,1)} %bitcast.17, bf16[7168,256]{1,0:T(8,128)(2,1)} %bitcast.18, ...), custom_call_target="tpu_custom_call" | custom-call | tf_op jit(solution)/shard_map/pallas_call | solution.py:308
  132.2 2.5 %copy.12 = bf16[96,7168]{1,0:T(8,128)(2,1)} copy(bf16[96,7168]{1,0:T(8,128)(2,1)} %shard_map.91) | data formatting | bytes 2752512
  (8 shorter events, 0.1 us)

commit v2 on v1

--- a/solution.py
+++ b/solution.py
@@ -33,9 +33,9 @@
 
 def kernel(n_e, n_d, tokens, fields, plan, gain, wg_hbm, wu_hbm, wd_hbm, out,
            wg, wu, wd, meta_out, meta_in, rows_out, rest_out, rows_in, rest_in,
-           acc, wide, send1, recv1, recv2, recv3, send4, recv4, gate, up,
+           acc, wide, send1, recv1, recv2, recv3, part_in, part_out, send4, recv4, gate, up,
            w_sem, meta_s, meta_r, rows_s, rows_r, rest_s, rest_r,
-           s1, r1, s2, r2, s3, r3, s4, r4):
+           s1, r1, s2, r2, s3, r3, sp, rp, s4, r4):
     e, d = lax.axis_index("expert"), lax.axis_index("dp")
     width = tokens.shape[1]
     cap = tokens.shape[0]
@@ -45,6 +45,11 @@
     chunks = width // CHUNK
     dps = [lax.rem(d + k, n_d) for k in range(1, n_d)]
     exs = [lax.rem(e + k, n_e) for k in range(1, n_e)]
+    half = n_d // 2
+    seat_of = lax.rem(d, half)
+    near_seats = [lax.rem(seat_of + k, half) for k in range(1, half)]
+    near = [d - seat_of + p for p in near_seats]
+    partner = lax.rem(d + half, n_d)
 
     def each_chunk(fn):
         def step(c, carry):
@@ -87,18 +92,37 @@
     pl.semaphore_wait(barrier, n_d - 1 + n_e - 1)
     meta_copies, row_copies, rest_copies = [], [], []
     for k, j in enumerate(dps):
-        def pack(cols, k=k):
-            block = dot(picks[k], tokens[:, cols]).astype(BF)
-            rows_out[k, :, cols] = block[:first]
-            if rest:
-                rest_out[k, :, cols] = block[first:]
         copy = remote(meta_out.at[k], meta_in.at[d], meta_s.at[k], meta_r.at[d], {"dp": j})
         copy.start()
         meta_copies.append(copy)
-        each_chunk(pack)
+    head = jnp.concatenate([p[:first] for p in picks])
+
+    def pack(cols):
+        rows_out[:, :, cols] = dot(head, tokens[:, cols]).astype(BF).reshape(n_d - 1, first, CHUNK)
+    each_chunk(pack)
+    for k, j in enumerate(dps):
         copy = remote(rows_out.at[k], rows_in.at[d], rows_s.at[k], rows_r.at[d], {"dp": j})
         copy.start()
         row_copies.append(copy)
+    if rest:
+        tail = jnp.concatenate([p[first:] for p in picks])
+
+        def pack_rest(cols):
+            rest_out[:, :, cols] = dot(tail, tokens[:, cols]).astype(BF).reshape(n_d - 1, rest, CHUNK)
+        each_chunk(pack_rest)
+    batch = 16
+
+    def rest_copy(k, j, slot, b):
+        rows = pl.ds(b * batch, batch)
+        return remote(rest_out.at[k, rows], rest_in.at[slot, rows],
+                      rest_s.at[b, k], rest_r.at[b, slot], {"dp": j})
+
+    def send_rest(b):
+        if b * batch < rest:
+            for k, j in enumerate(dps):
+                copy = rest_copy(k, j, d, b)
+                copy.start()
+                rest_copies.append(copy)
 
     def arrival(src, buf, sems, j, axis="dp"):
         return remote(src, buf.at[j], sems.at[j], sems.at[j], {axis: j})
@@ -149,6 +173,7 @@
     rows_in[d] = jnp.zeros(rows_in.shape[1:], BF)
     for k, j in enumerate(dps):
         arrival(rows_out.at[k], rows_in, rows_r, j).wait_recv()
+    send_rest(0)
 
     def named_part(cols):
         total = wide[:, cols]
@@ -184,15 +209,18 @@
     each_chunk(gather)
 
     two_copies = []
-    for k, j in enumerate(dps):
-        copy = remote(recv2.at[d], recv2.at[d], s2.at[k], r2.at[d], {"dp": j})
+    copy = remote(recv2.at[d], recv2.at[d], s2.at[0], r2.at[d], {"dp": partner})
+    copy.start()
+    two_copies.append(copy)
+    for k, j in enumerate(near):
+        copy = remote(recv2.at[d], recv2.at[d], s2.at[1 + k], r2.at[d], {"dp": j})
         copy.start()
         two_copies.append(copy)
-    if rest:
-        for k, j in enumerate(dps):
-            copy = remote(rest_out.at[k], rest_in.at[d], rest_s.at[k], rest_r.at[d], {"dp": j})
-            copy.start()
-            rest_copies.append(copy)
+    arrival(recv2.at[d], recv2, r2, partner).wait_recv()
+    for k, j in enumerate(near):
+        copy = remote(recv2.at[partner], recv2.at[partner], s2.at[half + k], r2.at[partner], {"dp": j})
+        copy.start()
+        two_copies.append(copy)
 
     def got_part(cols):
         total = acc[:, cols]
@@ -202,8 +230,10 @@
     each_chunk(got_part)
     for copy in loads:
         copy.wait()
-    for k, j in enumerate(dps):
+    for j in near:
         arrival(recv2.at[d], recv2, r2, j).wait_recv()
+        arrival(recv2.at[d], recv2, r2, lax.rem(j + half, n_d)).wait_recv()
+    send_rest(1)
 
     gate[...] = jnp.zeros_like(gate)
     up[...] = jnp.zeros_like(up)
@@ -223,17 +253,35 @@
         recv2[:, :, cols] = piece.reshape(n_d, slots, CHUNK)
     each_chunk(down)
     three_copies = []
-    for k, j in enumerate(dps):
-        copy = remote(recv2.at[j], recv3.at[d], s3.at[k], r3.at[d], {"dp": j})
+    for k, (j, p) in enumerate(zip(near, near_seats)):
+        copy = remote(recv2.at[lax.rem(j + half, n_d)], part_in.at[seat_of],
+                      sp.at[k], rp.at[seat_of], {"dp": j})
         copy.start()
         three_copies.append(copy)
-    for k, j in enumerate(dps):
-        arrival(recv2.at[j], recv3, r3, j).wait_recv()
+    for k, (j, p) in enumerate(zip(near, near_seats)):
+        copy = remote(recv2.at[j], recv3.at[seat_of], s3.at[k], r3.at[seat_of], {"dp": j})
+        copy.start()
+        three_copies.append(copy)
+    for p, j in zip(near_seats, near):
+        remote(recv2.at[j], part_in.at[p], sp.at[0], rp.at[p], {"dp": j}).wait_recv()
+
+    def partial_sum(cols):
+        total = recv2[partner, :, cols].astype(F32)
+        for p in near_seats:
+            total = total + part_in[p, :, cols].astype(F32)
+        part_out[:, cols] = total.astype(BF)
+    each_chunk(partial_sum)
+    copy = remote(part_out, recv3.at[half], s3.at[half - 1], r3.at[half], {"dp": partner})
+    copy.start()
+    three_copies.append(copy)
+    for p, j in zip(near_seats, near):
+        remote(recv2.at[j], recv3.at[p], s3.at[0], r3.at[p], {"dp": j}).wait_recv()
+    copy.wait_recv()
 
     def reduce(cols):
-        total = recv2[d, :, cols].astype(F32)
-        for j in dps:
-            total = total + recv3[j, :, cols].astype(F32)
+        total = recv2[d, :, cols].astype(F32) + recv3[half, :, cols].astype(F32)
+        for p in near_seats:
+            total = total + recv3[p, :, cols].astype(F32)
         wide[:, cols] = total
         for x in range(n_e):
             send4[x, :, cols] = wide[x * M:(x + 1) * M, cols].astype(BF)
@@ -248,8 +296,9 @@
 
     if rest:
         rest_in[d] = jnp.zeros(rest_in.shape[1:], BF)
-        for k, j in enumerate(dps):
-            arrival(rest_out.at[k], rest_in, rest_r, j).wait_recv()
+        for b in range(rest // batch):
+            for k, j in enumerate(dps):
+                rest_copy(k, j, j, b).wait_recv()
 
         def rest_part(cols):
             total = acc[:, cols]
@@ -325,7 +374,9 @@
             pltpu.VMEM((n_e, M, width), BF),
             pltpu.VMEM((n_e, M, width), BF),
             pltpu.VMEM((n_d, slots, width), BF),
-            pltpu.VMEM((n_d, slots, width), BF),
+            pltpu.VMEM((n_d // 2 + 1, slots, width), BF),
+            pltpu.VMEM((n_d // 2, slots, width), BF),
+            pltpu.VMEM((slots, width), BF),
             pltpu.VMEM((n_e, M, width), BF),
             pltpu.VMEM((n_e, M, width), BF),
             pltpu.VMEM((n_d * slots, part), F32),
@@ -333,8 +384,9 @@
             dma((3,)),
             dma((n_d,)), dma((n_d,)),
             dma((n_d,)), dma((n_d,)),
+            dma((2, n_d)), dma((2, n_d)),
+            dma((n_e,)), dma((n_e,)),
             dma((n_d,)), dma((n_d,)),
-            dma((n_e,)), dma((n_e,)),
             dma((n_d,)), dma((n_d,)),
             dma((n_d,)), dma((n_d,)),
             dma((n_e,)), dma((n_e,)),

time: 135 us -> 118 us (0.87)
  the two profiles are of different devices: /device:TPU:27 before, /device:TPU:0 now
where the time goes in v2:
time: 118 us; the launch traced here: 116 us
  Pallas kernels  103 us (87%)
  other arithmetic  4.72 us (4%)
  local copies, waits for them, and re-layouts  3.99 us (3%)
  between operations  3.93 us (3%)
    pallas_call x1, Pallas kernels, body(): pl.pallas_call(functools.partial(kernel, n_e, n_d), out_shape=jax.ShapeDt...  103 us
    unnamed x1, local copies, waits for them, and re-layouts  2.51 us

profile of v2, /device:TPU:0, one launch (start us, length us, event | category | flops | bytes accessed | tf_op | source)
XLA Modules:
  0.0 115.6 jit_solution(7847214946389380306)
XLA Ops:
  0.7 1.4 %reduce_sum.49 = s32[]{:T(128)} reduce(s32[1,4]{1,0:T(1,128)} %param.11, s32[]{:T(128)} %constant.10.clone.1), dimensions={0,1}, to_apply=%region_4.5 | reduce | flops 3 | bytes 24 | tf_op jit(solution)/shard_map/reduce_sum | solution.py:335
  2.7 1.5 %fusion.7 = (s32[1,1]{1,0:T(1,128)}, s32[1,1]{1,0:T(1,128)}, s32[1,1]{1,0:T(1,128)}, s32[1,1]{1,0:T(1,128)}) fusion(s32[1,4]{1,0:T(1,128)} %param.11), kind=kLoop, calls=%fused_computation.29 | loop fusion | bytes 32 | tf_op jit(solution)/shard_map/slice | solution.py:339
  6.8 0.7 fusion
  7.6 0.6 pad_maximum_fusion.1.plan
  8.2 0.6 pad_maximum_fusion.fields
  8.8 1.3 %broadcast_in_dim.69 = f32[7168]{0:T(1024)} convert(bf16[7168]{0:T(1024)(128)(2,1)} %param.14) | non-fusion elementwise | flops 7168 | bytes 43008 | tf_op jit(solution)/shard_map/broadcast_in_dim | solution.py:352
  10.1 103.0 %shard_map.91 = bf16[96,7168]{1,0:T(8,128)(2,1)} custom-call(bf16[144,7168]{1,0:T(8,128)(2,1)} %tokens.1, f32[24,256]{1,0:T(8,128)} %pad_maximum_fusion.fields, f32[8,256]{1,0:T(8,128)} %pad_maximum_fusion.1.plan, f32[1,7168]{1,0:T(1,128)} %bitcast.20, bf16[7168,256]{1,0:T(8,128)(2,1)} %bitcast.17, bf16[7168,256]{1,0:T(8,128)(2,1)} %bitcast.18, ...), custom_call_target="tpu_custom_call" | custom-call | tf_op jit(solution)/shard_map/pallas_call | solution.py:357
  113.1 2.5 %copy.12 = bf16[96,7168]{1,0:T(8,128)(2,1)} copy(bf16[96,7168]{1,0:T(8,128)(2,1)} %shard_map.91) | data formatting | bytes 2752512
  (8 shorter events, 0.1 us)

commit v3 on v2

--- a/solution.py
+++ b/solution.py
@@ -31,7 +31,7 @@
     return lax.broadcasted_iota(jnp.int32, shape, dim).astype(F32)
 
 
-def kernel(n_e, n_d, tokens, fields, plan, gain, wg_hbm, wu_hbm, wd_hbm, out,
+def kernel(n_e, n_d, counts, send_counts, tokens, routes, weights, gain, wg_hbm, wu_hbm, wd_hbm, out,
            wg, wu, wd, meta_out, meta_in, rows_out, rest_out, rows_in, rest_in,
            acc, wide, send1, recv1, recv2, recv3, part_in, part_out, send4, recv4, gate, up,
            w_sem, meta_s, meta_r, rows_s, rows_r, rest_s, rest_r,
@@ -73,9 +73,35 @@
     for x in exs:
         pl.semaphore_signal(barrier, inc=1, device_id={"expert": x}, device_id_type=MESH)
 
-    lanes = plan.shape[1]
+    lanes = -(-cap // LANES) * LANES
+    ids, values = routes[...], weights[...].astype(F32)
+    expert_of = lax.broadcasted_iota(jnp.int32, (1, LANES), 1) // M
+    chosen = jnp.zeros((cap, LANES), F32)
+    for x in range(n_e):
+        column = jnp.sum(jnp.where(ids == x, values, 0.0), axis=1, keepdims=True)
+        chosen = chosen + column * (expert_of == x).astype(F32)
+    chosen = jnp.concatenate([chosen, jnp.zeros((lanes - cap, LANES), F32)])
+    place_ids = lax.broadcasted_iota(jnp.int32, (1, lanes), 1)
+    begin = counts[0]
+    for j in range(n_d):
+        begin = begin - send_counts[0, j]
+    target = jnp.where(place_ids < begin, -1, -2)
+    index = place_ids
+    for j in range(n_d):
+        after = begin + send_counts[0, j]
+        inside = (place_ids >= begin) & (place_ids < after)
+        target = jnp.where(inside, j, target)
+        index = jnp.where(inside, place_ids - begin, index)
+        begin = after
+    target = target.astype(F32)
+    valid = (target > -2.0).astype(F32)
+    eye = (iota((slots, LANES), 0) == iota((slots, LANES), 1)).astype(F32)
+    chosen = dot_nt(eye, chosen) * valid
+    named = (jnp.max(chosen, axis=0, keepdims=True) > 0).astype(F32)
+    low = iota((8, lanes), 0)
+    fields = jnp.concatenate([
+        chosen, jnp.where(low == 0, valid, jnp.where(low == 1, index.astype(F32), 0.0))])
     upper = (iota((lanes, lanes), 0) < iota((lanes, lanes), 1)).astype(BF)
-    target, named = plan[0:1, :], plan[1:2, :]
     picks = []
     for k, j in enumerate(dps):
         mine = (target == j.astype(F32)).astype(F32)
@@ -86,7 +112,7 @@
         total = jnp.sum(ahead, axis=1, keepdims=True)
         slot = jnp.where(ahead > 0, before_a, jnp.where(behind > 0, total + before_b, -1.0))
         pick = (iota((LANES, lanes), 0) == slot).astype(F32)
-        meta_out[k] = dot_nt(fields[...], pick)
+        meta_out[k] = dot_nt(fields, pick)
         picks.append(pick.astype(BF)[:T_MAX, :cap])
 
     pl.semaphore_wait(barrier, n_d - 1 + n_e - 1)
@@ -117,9 +143,12 @@
         return remote(rest_out.at[k, rows], rest_in.at[slot, rows],
                       rest_s.at[b, k], rest_r.at[b, slot], {"dp": j})
 
-    def send_rest(b):
+    across = [lax.rem(j + half, n_d) for j in near]
+
+    def send_rest(b, peers):
         if b * batch < rest:
-            for k, j in enumerate(dps):
+            for j in peers:
+                k = lax.rem(j - d - 1 + 2 * n_d, n_d)
                 copy = rest_copy(k, j, d, b)
                 copy.start()
                 rest_copies.append(copy)
@@ -129,7 +158,7 @@
 
     own = (target == -1.0).astype(F32)
     kept = jnp.sum(own, axis=1, keepdims=True)
-    own_f = fields[...] * own
+    own_f = fields * own
     rank_of = lax.broadcasted_iota(jnp.int32, (slots, 1), 0) % M
     rank_of = rank_of.astype(F32)
     base = jnp.zeros((slots, 1), F32)
@@ -173,7 +202,7 @@
     rows_in[d] = jnp.zeros(rows_in.shape[1:], BF)
     for k, j in enumerate(dps):
         arrival(rows_out.at[k], rows_in, rows_r, j).wait_recv()
-    send_rest(0)
+    send_rest(0, [partner] + near)
 
     def named_part(cols):
         total = wide[:, cols]
@@ -188,7 +217,7 @@
     scale = lax.rsqrt(lax.fori_loop(0, chunks, squares, jnp.zeros((slots, 1), F32)) / width + EPSILON)
 
     def norm(cols):
-        wide[:, cols] = wide[:, cols] * scale * gain[:, cols]
+        wide[:, cols] = wide[:, cols] * scale * gain[:, cols].astype(F32)
         for x in range(n_e):
             send1[x, :, cols] = wide[x * M:(x + 1) * M, cols].astype(BF)
     each_chunk(norm)
@@ -233,7 +262,7 @@
     for j in near:
         arrival(recv2.at[d], recv2, r2, j).wait_recv()
         arrival(recv2.at[d], recv2, r2, lax.rem(j + half, n_d)).wait_recv()
-    send_rest(1)
+    send_rest(0, across)
 
     gate[...] = jnp.zeros_like(gate)
     up[...] = jnp.zeros_like(up)
@@ -262,6 +291,7 @@
         copy = remote(recv2.at[j], recv3.at[seat_of], s3.at[k], r3.at[seat_of], {"dp": j})
         copy.start()
         three_copies.append(copy)
+    send_rest(1, [partner])
     for p, j in zip(near_seats, near):
         remote(recv2.at[j], part_in.at[p], sp.at[0], rp.at[p], {"dp": j}).wait_recv()
 
@@ -274,6 +304,7 @@
     copy = remote(part_out, recv3.at[half], s3.at[half - 1], r3.at[half], {"dp": partner})
     copy.start()
     three_copies.append(copy)
+    send_rest(1, across + near)
     for p, j in zip(near_seats, near):
         remote(recv2.at[j], recv3.at[p], s3.at[0], r3.at[p], {"dp": j}).wait_recv()
     copy.wait_recv()
@@ -326,38 +357,16 @@
     slots = n_e * M
     first = min(T_MAX, slots)
     rest = T_MAX - first
-    lanes = -(-cap // LANES) * LANES
-    pad = ((0, 0), (0, lanes - cap))
-    ids = jnp.pad(routes.T, pad, constant_values=-1)
-    weights = jnp.pad(route_weights.T.astype(F32), pad)
-    place = jnp.arange(lanes, dtype=jnp.int32)
-    send_row = send_counts[0]
-    begin = counts[0] - jnp.sum(send_row)
-    target = jnp.where(place < begin, -1, -2)
-    index = place
-    for j in range(n_d):
-        inside = (place >= begin) & (place < begin + send_row[j])
-        target = jnp.where(inside, j, target)
-        index = jnp.where(inside, place - begin, index)
-        begin = begin + send_row[j]
-    valid = (target > -2).astype(F32)
-    chosen = jnp.stack(
-        [jnp.sum(jnp.where(ids == x, weights, 0.0), axis=0) for x in range(n_e)]) * valid
-    named = jnp.any(chosen > 0, axis=0).astype(F32)
-    height = -(-(slots + 2) // 8) * 8
-    fields = jnp.concatenate([
-        jnp.repeat(chosen, M, axis=0), valid[None], index.astype(F32)[None],
-        jnp.zeros((height - slots - 2, lanes), F32)])
-    plan = jnp.concatenate([target.astype(F32)[None], named[None], jnp.zeros((6, lanes), F32)])
-    gain = norm_gain.astype(F32)[None]
+    height = slots + 8
 
     vmem = pl.BlockSpec(memory_space=pltpu.VMEM)
+    smem = pl.BlockSpec(memory_space=pltpu.SMEM)
     hbm = pl.BlockSpec(memory_space=pl.ANY)
     dma = pltpu.SemaphoreType.DMA
     return pl.pallas_call(
         functools.partial(kernel, n_e, n_d),
         out_shape=jax.ShapeDtypeStruct((BAL, width), BF),
-        in_specs=[vmem] * 4 + [hbm] * 3,
+        in_specs=[smem] * 2 + [vmem] * 4 + [hbm] * 3,
         out_specs=vmem,
         scratch_shapes=[
             pltpu.VMEM((width, part), BF),
@@ -393,7 +402,7 @@
         ],
         compiler_params=pltpu.CompilerParams(
             collective_id=0, has_side_effects=True, vmem_limit_bytes=60 * 1024 * 1024),
-    )(tokens, fields, plan, gain, w_gate[0], w_up[0], w_down[0])
+    )(counts, send_counts, tokens, routes, route_weights, norm_gain[None], w_gate[0], w_up[0], w_down[0])
 
 
 def solution(mesh):

time: 118 us -> 111 us (0.941); the launches traced: 116 us -> 111 us
  other arithmetic: 4.72 us -> 0 us
  between operations: 3.93 us -> 0.66 us
  local copies, waits for them, and re-layouts: 3.99 us -> 6.68 us
    unnamed x1 -> x3, local copies, waits for them, and re-layouts: 2.51 us -> 5.34 us
    reduce_sum x2 -> x0, other arithmetic: 2.1 us -> none  [the longest x1 1.38 us: body(): begin = counts[0] - jnp.sum(send_row)]
    slice x1 -> x0, local copies, waits for them, and re-layouts: 1.47 us -> none  [body(): inside = (place >= begin) & (place < begin + send_row[j])]
    broadcast_in_dim x1, local copies, waits for them, and re-layouts: 0.01 us -> 1.33 us  [body(): norm_gain[None]]
    broadcast_in_dim x1 -> x0, other arithmetic: 1.32 us -> none  [body(): gain = norm_gain.astype(F32)[None]]
    concatenate x2 -> x0, other arithmetic: 1.22 us -> none  [the longest x1 0.61 us: body(): jnp.concatenate([jnp.repeat(chosen, M, axis=0), valid[None], index.astype...]
where the time goes in v3:
time: 111 us
  Pallas kernels  104 us (94%)
  local copies, waits for them, and re-layouts  6.68 us (6%)
    pallas_call x1, Pallas kernels, body(): pl.pallas_call(functools.partial(kernel, n_e, n_d), out_shape=jax.ShapeDt...  104 us
    unnamed x3, local copies, waits for them, and re-layouts  5.34 us

profile of v3, /device:TPU:0, one launch (start us, length us, event | category | flops | bytes accessed | tf_op | source)
XLA Modules:
  0.0 110.9 jit_solution(1634518845355564571)
XLA Ops:
  0.7 1.3 %broadcast_in_dim.3.gain = bf16[1,7168]{1,0:T(2,128)(2,1)} reshape(bf16[7168]{0:T(1024)(128)(2,1)} %param.14) | data formatting | bytes 28672 | tf_op jit(solution)/shard_map/broadcast_in_dim | solution.py:405
  2.0 1.4 %copy.11.weights = bf16[144,8]{1,0:T(8,128)(2,1)} copy(bf16[144,8]{0,1:T(8,128)(2,1)} %param.13) | data formatting | bytes 4608 | tf_op args[4]
  3.4 1.4 %copy.10.routes = s32[144,8]{1,0:T(8,128)} copy(s32[144,8]{0,1:T(8,128)} %param.12) | data formatting | bytes 9216 | tf_op args[3]
  4.8 103.6 %shard_map.91 = bf16[96,7168]{1,0:T(8,128)(2,1)} custom-call(s32[1]{0:T(128)S(6)} %copy.13.counts, s32[1,4]{1,0:T(1,128)} %send_counts.1, bf16[144,7168]{1,0:T(8,128)(2,1)} %tokens.1, s32[144,8]{1,0:T(8,128)} %copy.10.routes, bf16[144,8]{1,0:T(8,128)(2,1)} %copy.11.weights, bf16[1,7168]{1,0:T(2,128)(2,1)} %broadcast_in_dim.3.gain, ...), custom_call_target="tpu_custom_call" | custom-call | tf_op jit(solution)/shard_map/pallas_call | solution.py:366
  108.4 2.5 %copy.14 = bf16[96,7168]{1,0:T(8,128)(2,1)} copy(bf16[96,7168]{1,0:T(8,128)(2,1)} %shard_map.91) | data formatting | bytes 2752512

commit v4 on v3

--- a/solution.py
+++ b/solution.py
@@ -11,7 +11,8 @@
 M = 4
 EPSILON = 1e-06
 LANES = 128
-CHUNK = 1024
+CHUNK = 3584
+PARTS = 2
 MESH = pl.DeviceIdType.MESH
 BF = jnp.bfloat16
 F32 = jnp.float32
@@ -51,11 +52,15 @@
     near = [d - seat_of + p for p in near_seats]
     partner = lax.rem(d + half, n_d)
 
-    def each_chunk(fn):
+    per_part = chunks // PARTS
+    parts = [pl.ds(q * (width // PARTS), width // PARTS) for q in range(PARTS)]
+
+    def each_chunk(fn, q=None):
         def step(c, carry):
             fn(pl.ds(pl.multiple_of(c * CHUNK, CHUNK), CHUNK))
             return carry
-        lax.fori_loop(0, chunks, step, 0)
+        lo, hi = (0, chunks) if q is None else (q * per_part, (q + 1) * per_part)
+        lax.fori_loop(lo, hi, step, 0)
 
     def remote(src, dst, send, recv, device):
         return pltpu.make_async_remote_copy(
@@ -75,12 +80,11 @@
 
     lanes = -(-cap // LANES) * LANES
     ids, values = routes[...], weights[...].astype(F32)
-    expert_of = lax.broadcasted_iota(jnp.int32, (1, LANES), 1) // M
-    chosen = jnp.zeros((cap, LANES), F32)
+    wide_pad = jnp.zeros((1, lanes - cap), F32)
+    picked = []
     for x in range(n_e):
-        column = jnp.sum(jnp.where(ids == x, values, 0.0), axis=1, keepdims=True)
-        chosen = chosen + column * (expert_of == x).astype(F32)
-    chosen = jnp.concatenate([chosen, jnp.zeros((lanes - cap, LANES), F32)])
+        row = jnp.sum(jnp.where(ids == x, values, 0.0), axis=0, keepdims=True)
+        picked.append(jnp.concatenate([row, wide_pad], axis=1))
     place_ids = lax.broadcasted_iota(jnp.int32, (1, lanes), 1)
     begin = counts[0]
     for j in range(n_d):
@@ -95,8 +99,10 @@
         begin = after
     target = target.astype(F32)
     valid = (target > -2.0).astype(F32)
-    eye = (iota((slots, LANES), 0) == iota((slots, LANES), 1)).astype(F32)
-    chosen = dot_nt(eye, chosen) * valid
+    owner = lax.broadcasted_iota(jnp.int32, (slots, 1), 0) // M
+    chosen = jnp.zeros((slots, lanes), F32)
+    for x in range(n_e):
+        chosen = jnp.where(owner == x, picked[x] * valid, chosen)
     named = (jnp.max(chosen, axis=0, keepdims=True) > 0).astype(F32)
     low = iota((8, lanes), 0)
     fields = jnp.concatenate([
@@ -217,39 +223,39 @@
     scale = lax.rsqrt(lax.fori_loop(0, chunks, squares, jnp.zeros((slots, 1), F32)) / width + EPSILON)
 
     def norm(cols):
-        wide[:, cols] = wide[:, cols] * scale * gain[:, cols].astype(F32)
+        wide[:, cols] = wide[:, cols] * scale * gain[cols].astype(F32).reshape(1, CHUNK)
         for x in range(n_e):
             send1[x, :, cols] = wide[x * M:(x + 1) * M, cols].astype(BF)
-    each_chunk(norm)
-
     one_copies = []
-    for k, x in enumerate(exs):
-        copy = remote(send1.at[x], recv1.at[e], s1.at[k], r1.at[e], {"expert": x})
-        copy.start()
-        one_copies.append(copy)
+    for q, cols in enumerate(parts):
+        each_chunk(norm, q)
+        for k, x in enumerate(exs):
+            copy = remote(send1.at[x, :, cols], recv1.at[e, :, cols],
+                          s1.at[q, k], r1.at[q, e], {"expert": x})
+            copy.start()
+            one_copies.append(copy)
     recv1[e] = send1[e]
-    for k, x in enumerate(exs):
-        arrival(send1.at[x], recv1, r1, x, "expert").wait_recv()
 
     def gather(cols):
         for x in range(n_e):
             wide[x * M:(x + 1) * M, cols] = recv1[x, :, cols].astype(F32)
         recv2[d, :, cols] = wide[:, cols].astype(BF)
-    each_chunk(gather)
 
     two_copies = []
-    copy = remote(recv2.at[d], recv2.at[d], s2.at[0], r2.at[d], {"dp": partner})
-    copy.start()
-    two_copies.append(copy)
-    for k, j in enumerate(near):
-        copy = remote(recv2.at[d], recv2.at[d], s2.at[1 + k], r2.at[d], {"dp": j})
-        copy.start()
-        two_copies.append(copy)
-    arrival(recv2.at[d], recv2, r2, partner).wait_recv()
-    for k, j in enumerate(near):
-        copy = remote(recv2.at[partner], recv2.at[partner], s2.at[half + k], r2.at[partner], {"dp": j})
-        copy.start()
-        two_copies.append(copy)
+
+    def block_copy(q, block, k, j):
+        ref = recv2.at[block, :, parts[q]]
+        return remote(ref, ref, s2.at[q, k], r2.at[q, block], {"dp": j})
+
+    for q, cols in enumerate(parts):
+        for k, x in enumerate(exs):
+            remote(send1.at[x, :, cols], recv1.at[x, :, cols],
+                   s1.at[q, k], r1.at[q, x], {"expert": x}).wait_recv()
+        each_chunk(gather, q)
+        for k, j in enumerate([partner] + near):
+            copy = block_copy(q, d, k, j)
+            copy.start()
+            two_copies.append(copy)
 
     def got_part(cols):
         total = acc[:, cols]
@@ -259,11 +265,6 @@
     each_chunk(got_part)
     for copy in loads:
         copy.wait()
-    for j in near:
-        arrival(recv2.at[d], recv2, r2, j).wait_recv()
-        arrival(recv2.at[d], recv2, r2, lax.rem(j + half, n_d)).wait_recv()
-    send_rest(0, across)
-
     gate[...] = jnp.zeros_like(gate)
     up[...] = jnp.zeros_like(up)
 
@@ -271,7 +272,19 @@
         x = recv2[:, :, cols].reshape(n_d * slots, CHUNK)
         gate[...] += dot(x, wg[cols, :])
         up[...] += dot(x, wu[cols, :])
-    each_chunk(project)
+    for q in range(PARTS):
+        block_copy(q, partner, 0, partner).wait_recv()
+        for k, j in enumerate(near):
+            copy = block_copy(q, partner, half + k, j)
+            copy.start()
+            two_copies.append(copy)
+    for q in range(PARTS):
+        for j in near:
+            block_copy(q, j, 0, j).wait_recv()
+            block_copy(q, lax.rem(j + half, n_d), 0, j).wait_recv()
+        if q == PARTS - 1:
+            send_rest(0, across)
+        each_chunk(project, q)
     g = gate[...]
     hidden = (g / (1.0 + jnp.exp(-g)) * up[...]).astype(BF)
     for copy in two_copies:
@@ -280,34 +293,45 @@
     def down(cols):
         piece = dot(hidden, wd[:, cols]).astype(BF)
         recv2[:, :, cols] = piece.reshape(n_d, slots, CHUNK)
-    each_chunk(down)
     three_copies = []
-    for k, (j, p) in enumerate(zip(near, near_seats)):
-        copy = remote(recv2.at[lax.rem(j + half, n_d)], part_in.at[seat_of],
-                      sp.at[k], rp.at[seat_of], {"dp": j})
-        copy.start()
-        three_copies.append(copy)
-    for k, (j, p) in enumerate(zip(near, near_seats)):
-        copy = remote(recv2.at[j], recv3.at[seat_of], s3.at[k], r3.at[seat_of], {"dp": j})
-        copy.start()
-        three_copies.append(copy)
+
+    def part_copy(q, j, k, p):
+        return remote(recv2.at[lax.rem(j + half, n_d), :, parts[q]], part_in.at[p, :, parts[q]],
+                      sp.at[q, k], rp.at[q, p], {"dp": j})
+
+    def near_copy(q, j, k, p):
+        return remote(recv2.at[j, :, parts[q]], recv3.at[p, :, parts[q]],
+                      s3.at[q, k], r3.at[q, p], {"dp": j})
+
+    def far_copy(q):
+        return remote(part_out.at[:, parts[q]], recv3.at[half, :, parts[q]],
+                      s3.at[q, half - 1], r3.at[q, half], {"dp": partner})
+
+    for q in range(PARTS):
+        each_chunk(down, q)
+        for k, j in enumerate(near):
+            copy = part_copy(q, j, k, seat_of)
+            copy.start()
+            three_copies.append(copy)
     send_rest(1, [partner])
-    for p, j in zip(near_seats, near):
-        remote(recv2.at[j], part_in.at[p], sp.at[0], rp.at[p], {"dp": j}).wait_recv()
 
     def partial_sum(cols):
         total = recv2[partner, :, cols].astype(F32)
         for p in near_seats:
             total = total + part_in[p, :, cols].astype(F32)
         part_out[:, cols] = total.astype(BF)
-    each_chunk(partial_sum)
-    copy = remote(part_out, recv3.at[half], s3.at[half - 1], r3.at[half], {"dp": partner})
-    copy.start()
-    three_copies.append(copy)
+    for q in range(PARTS):
+        for p, j in zip(near_seats, near):
+            part_copy(q, j, 0, p).wait_recv()
+        each_chunk(partial_sum, q)
+        copy = far_copy(q)
+        copy.start()
+        three_copies.append(copy)
+        for k, j in enumerate(near):
+            copy = near_copy(q, j, k, seat_of)
+            copy.start()
+            three_copies.append(copy)
     send_rest(1, across + near)
-    for p, j in zip(near_seats, near):
-        remote(recv2.at[j], recv3.at[p], s3.at[0], r3.at[p], {"dp": j}).wait_recv()
-    copy.wait_recv()
 
     def reduce(cols):
         total = recv2[d, :, cols].astype(F32) + recv3[half, :, cols].astype(F32)
@@ -316,13 +340,22 @@
         wide[:, cols] = total
         for x in range(n_e):
             send4[x, :, cols] = wide[x * M:(x + 1) * M, cols].astype(BF)
-    each_chunk(reduce)
 
     four_copies = []
-    for k, x in enumerate(exs):
-        copy = remote(send4.at[x], recv4.at[e], s4.at[k], r4.at[e], {"expert": x})
-        copy.start()
-        four_copies.append(copy)
+
+    def back_copy(q, x, k, slot):
+        return remote(send4.at[x, :, parts[q]], recv4.at[slot, :, parts[q]],
+                      s4.at[q, k], r4.at[q, slot], {"expert": x})
+
+    for q in range(PARTS):
+        for p, j in zip(near_seats, near):
+            near_copy(q, j, 0, p).wait_recv()
+        far_copy(q).wait_recv()
+        each_chunk(reduce, q)
+        for k, x in enumerate(exs):
+            copy = back_copy(q, x, k, e)
+            copy.start()
+            four_copies.append(copy)
     recv4[e] = send4[e]
 
     if rest:
@@ -337,15 +370,16 @@
                 total = total + dot(seats[j][:, first:], rest_in[j, :, cols])
             acc[:, cols] = total
         each_chunk(rest_part)
-    for k, x in enumerate(exs):
-        arrival(send4.at[x], recv4, r4, x, "expert").wait_recv()
     table = table.astype(BF)
 
     def finish(cols):
         for x in range(n_e):
             wide[x * M:(x + 1) * M, cols] = recv4[x, :, cols].astype(F32)
         out[:, cols] = (acc[:, cols] + dot(table, wide[:, cols])).astype(BF)
-    each_chunk(finish)
+    for q in range(PARTS):
+        for k, x in enumerate(exs):
+            back_copy(q, x, k, x).wait_recv()
+        each_chunk(finish, q)
     for copy in meta_copies + row_copies + rest_copies + one_copies + three_copies + four_copies:
         copy.wait_send()
 
@@ -394,15 +428,15 @@
             dma((n_d,)), dma((n_d,)),
             dma((n_d,)), dma((n_d,)),
             dma((2, n_d)), dma((2, n_d)),
-            dma((n_e,)), dma((n_e,)),
-            dma((n_d,)), dma((n_d,)),
-            dma((n_d,)), dma((n_d,)),
-            dma((n_d,)), dma((n_d,)),
-            dma((n_e,)), dma((n_e,)),
+            dma((PARTS, n_e)), dma((PARTS, n_e)),
+            dma((PARTS, n_d)), dma((PARTS, n_d)),
+            dma((PARTS, n_d)), dma((PARTS, n_d)),
+            dma((PARTS, n_d)), dma((PARTS, n_d)),
+            dma((PARTS, n_e)), dma((PARTS, n_e)),
         ],
         compiler_params=pltpu.CompilerParams(
             collective_id=0, has_side_effects=True, vmem_limit_bytes=60 * 1024 * 1024),
-    )(counts, send_counts, tokens, routes, route_weights, norm_gain[None], w_gate[0], w_up[0], w_down[0])
+    )(counts, send_counts, tokens, routes.T, route_weights.T, norm_gain, w_gate[0], w_up[0], w_down[0])
 
 
 def solution(mesh):

time: 111 us -> 105 us (0.946)
  local copies, waits for them, and re-layouts: 6.68 us -> 2.51 us
  Pallas kernels: 104 us -> 102 us
    unnamed x3 -> x1, local copies, waits for them, and re-layouts: 5.34 us -> 2.51 us
    pallas_call x1, Pallas kernels: 104 us -> 102 us  [body(): pl.pallas_call(functools.partial(kernel, n_e, n_d), out_shape=jax.ShapeDt...]
    broadcast_in_dim x1 -> x0, local copies, waits for them, and re-layouts: 1.33 us -> none  [body(): norm_gain[None]]
where the time goes in v4:
time: 105 us
  Pallas kernels  102 us (97%)
  local copies, waits for them, and re-layouts  2.51 us (2%)
    pallas_call x1, Pallas kernels, body(): pl.pallas_call(functools.partial(kernel, n_e, n_d), out_shape=jax.ShapeDt...  102 us
    unnamed x1, local copies, waits for them, and re-layouts  2.51 us

profile of v4, /device:TPU:0, one launch (start us, length us, event | category | flops | bytes accessed | tf_op | source)
XLA Modules:
  0.0 104.8 jit_solution(11859146943635244385)
XLA Ops:
  0.7 101.7 %shard_map.91 = bf16[96,7168]{1,0:T(8,128)(2,1)} custom-call(s32[1]{0:T(128)S(6)} %copy.11.counts, s32[1,4]{1,0:T(1,128)} %send_counts.1, bf16[144,7168]{1,0:T(8,128)(2,1)} %tokens.1, s32[8,144]{1,0:T(8,128)} %bitcast.8, bf16[8,144]{1,0:T(8,128)(2,1)} %bitcast.9, bf16[7168]{0:T(1024)(128)(2,1)} %gain.1, bf16[7168,256]{1,0:T(8,128)(2,1)} %bitcast.5, ...), custom_call_target="tpu_custom_call" | custom-call | tf_op jit(solution)/shard_map/pallas_call | solution.py:400
  102.3 2.5 %copy.12 = bf16[96,7168]{1,0:T(8,128)(2,1)} copy(bf16[96,7168]{1,0:T(8,128)(2,1)} %shard_map.91) | data formatting | bytes 2752512

commit v5 on v4

--- a/solution.py
+++ b/solution.py
@@ -132,7 +132,9 @@
     def pack(cols):
         rows_out[:, :, cols] = dot(head, tokens[:, cols]).astype(BF).reshape(n_d - 1, first, CHUNK)
     each_chunk(pack)
-    for k, j in enumerate(dps):
+    across = [lax.rem(j + half, n_d) for j in near]
+    for j in across + [partner] + near:
+        k = lax.rem(j - d - 1 + 2 * n_d, n_d)
         copy = remote(rows_out.at[k], rows_in.at[d], rows_s.at[k], rows_r.at[d], {"dp": j})
         copy.start()
         row_copies.append(copy)
@@ -148,8 +150,6 @@
         rows = pl.ds(b * batch, batch)
         return remote(rest_out.at[k, rows], rest_in.at[slot, rows],
                       rest_s.at[b, k], rest_r.at[b, slot], {"dp": j})
-
-    across = [lax.rem(j + half, n_d) for j in near]
 
     def send_rest(b, peers):
         if b * batch < rest:
@@ -202,19 +202,21 @@
         offset = offset + jnp.sum(valid, axis=1, keepdims=True)
         a = (iota((BAL, LANES), 0) == seat).astype(F32)
         table = table + dot_nt(a, placed * f[:slots])
-        seats.append(a.astype(BF)[:, :T_MAX])
-        places.append(placed.astype(BF)[:, :first])
-
+        seats.append(a[:, :T_MAX])
+        places.append(placed[:, :first])
+
+    place_all = jnp.concatenate(places, axis=1).astype(BF)
+    seat_head = jnp.concatenate([a[:, :first] for a in seats], axis=1).astype(BF)
+    if rest:
+        seat_tail = jnp.concatenate([a[:, first:] for a in seats], axis=1).astype(BF)
     rows_in[d] = jnp.zeros(rows_in.shape[1:], BF)
     for k, j in enumerate(dps):
         arrival(rows_out.at[k], rows_in, rows_r, j).wait_recv()
     send_rest(0, [partner] + near)
 
     def named_part(cols):
-        total = wide[:, cols]
-        for j in range(n_d):
-            total = total + dot(places[j], rows_in[j, :, cols])
-        wide[:, cols] = total
+        block = rows_in[:, :, cols].reshape(n_d * first, CHUNK)
+        wide[:, cols] += dot(place_all, block)
     each_chunk(named_part)
 
     def squares(c, carry):
@@ -258,10 +260,8 @@
             two_copies.append(copy)
 
     def got_part(cols):
-        total = acc[:, cols]
-        for j in range(n_d):
-            total = total + dot(seats[j][:, :first], rows_in[j, :, cols])
-        acc[:, cols] = total
+        block = rows_in[:, :, cols].reshape(n_d * first, CHUNK)
+        acc[:, cols] += dot(seat_head, block)
     each_chunk(got_part)
     for copy in loads:
         copy.wait()
@@ -284,6 +284,7 @@
             block_copy(q, lax.rem(j + half, n_d), 0, j).wait_recv()
         if q == PARTS - 1:
             send_rest(0, across)
+            send_rest(1, [partner])
         each_chunk(project, q)
     g = gate[...]
     hidden = (g / (1.0 + jnp.exp(-g)) * up[...]).astype(BF)
@@ -313,7 +314,6 @@
             copy = part_copy(q, j, k, seat_of)
             copy.start()
             three_copies.append(copy)
-    send_rest(1, [partner])
 
     def partial_sum(cols):
         total = recv2[partner, :, cols].astype(F32)
@@ -365,10 +365,8 @@
                 rest_copy(k, j, j, b).wait_recv()
 
         def rest_part(cols):
-            total = acc[:, cols]
-            for j in range(n_d):
-                total = total + dot(seats[j][:, first:], rest_in[j, :, cols])
-            acc[:, cols] = total
+            block = rest_in[:, :, cols].reshape(n_d * rest, CHUNK)
+            acc[:, cols] += dot(seat_tail, block)
         each_chunk(rest_part)
     table = table.astype(BF)
 

time: 105 us -> 101 us (0.962)
  Pallas kernels: 102 us -> 97.7 us
    pallas_call x1, Pallas kernels: 102 us -> 97.7 us  [body(): pl.pallas_call(functools.partial(kernel, n_e, n_d), out_shape=jax.ShapeDt...]
where the time goes in v5:
time: 101 us
  Pallas kernels  97.7 us (97%)
  local copies, waits for them, and re-layouts  2.51 us (2%)
    pallas_call x1, Pallas kernels, body(): pl.pallas_call(functools.partial(kernel, n_e, n_d), out_shape=jax.ShapeDt...  97.7 us
    unnamed x1, local copies, waits for them, and re-layouts  2.51 us

profile of v5, /device:TPU:0, one launch (start us, length us, event | category | flops | bytes accessed | tf_op | source)
XLA Modules:
  0.0 100.8 jit_solution(13805919937068271495)
XLA Ops:
  0.7 97.7 %shard_map.91 = bf16[96,7168]{1,0:T(8,128)(2,1)} custom-call(s32[1]{0:T(128)S(6)} %copy.11.counts, s32[1,4]{1,0:T(1,128)} %send_counts.1, bf16[144,7168]{1,0:T(8,128)(2,1)} %tokens.1, s32[8,144]{1,0:T(8,128)} %bitcast.8, bf16[8,144]{1,0:T(8,128)(2,1)} %bitcast.9, bf16[7168]{0:T(1024)(128)(2,1)} %gain.1, bf16[7168,256]{1,0:T(8,128)(2,1)} %bitcast.5, ...), custom_call_target="tpu_custom_call" | custom-call | tf_op jit(solution)/shard_map/pallas_call | solution.py:398
  98.3 2.5 %copy.12 = bf16[96,7168]{1,0:T(8,128)(2,1)} copy(bf16[96,7168]{1,0:T(8,128)(2,1)} %shard_map.91) | data formatting | bytes 2752512
